TPU v7x, 256 devices: a whole 4x4x8 slice. The times are simulated.
256 devices in a mesh: seq: 64 (over y, z, core), tp: 4 (over x).
Axes of the slice: x: 4, y: 4, z: 8, core: 2. Of those that a mesh axis runs over, the one named last changes fastest.
Arguments:
- signal: float32 [32, 1048576], P(None, ('seq', 'tp')), may hold values from -6 to 6
- filter_taps: float32 [32, 1048576], P(None, ('seq', 'tp')), as said below
- skip_gain: float32 [32], P('tp'), may hold values from -4 to 4
Outputs:
- output: float32 [32, 1048576], P('tp', 'seq')
Inputs may be any that keep to these rules, and one draw needn't show every extreme that they name: `filter_taps`: filter taps are real values of both signs.
All inputs are finite; a program needn't handle non-finite values.
Results may differ from a plain program's by a relative error of at most 0.000082.
Values sent between devices are 32-bit elements; how exact they have to be, the bound alone decides.
No kernel may reach another device: no remote copies, remote signals or barrier semaphores. Data moves between devices by JAX's collectives and lax.ppermute only.
A program may use at most 64 MiB of HBM per device.

v0:
```python
import math
import jax
import jax.numpy as jnp
from jax import lax
from jax.sharding import PartitionSpec as P

HIGHEST = lax.Precision.HIGHEST
block_radix = 128


def phase_table(product, modulus):
    angle = (product % modulus).astype(jnp.float32) * (2.0 * math.pi / modulus)
    return (jnp.cos(angle), jnp.sin(angle))


def rotate_sum(pattern, spectrum, tables, turn_sign):
    real_part, imag_part = spectrum
    cosine, sine_table = tables
    cos_real = jnp.einsum(pattern, real_part, cosine, precision=HIGHEST)
    cos_imag = jnp.einsum(pattern, imag_part, cosine, precision=HIGHEST)
    sin_real = jnp.einsum(pattern, real_part, sine_table, precision=HIGHEST)
    sin_imag = jnp.einsum(pattern, imag_part, sine_table, precision=HIGHEST)
    return (cos_real - turn_sign * sin_imag, cos_imag + turn_sign * sin_real)


def rotate(spectrum, tables, turn_sign):
    real_part, imag_part = spectrum
    cosine, sine_table = tables
    return (
        real_part * cosine - turn_sign * imag_part * sine_table,
        imag_part * cosine + turn_sign * real_part * sine_table,
    )


def body(signal, filter_taps, skip_gain):
    seq_count = lax.axis_size("seq")
    seq_index = lax.axis_index("seq")
    tp_count = lax.axis_size("tp")
    channels = signal.shape[0] // tp_count
    slab_signal, slab_filter = (
        lax.all_to_all(signal, "tp", split_axis=0, concat_axis=1, tiled=True),
        lax.all_to_all(filter_taps, "tp", split_axis=0, concat_axis=1, tiled=True),
    )
    slab_rows = jnp.concatenate([slab_signal, slab_filter], axis=0)
    all_rows = slab_rows.shape[0]
    tokens = slab_rows.shape[1]
    block_width = tokens // seq_count
    freq_rows = 2 * seq_count
    fft_length = freq_rows * tokens
    inner_count = tokens // block_radix
    row_index = jnp.arange(freq_rows, dtype=jnp.int32)
    token_index = jnp.arange(block_width, dtype=jnp.int32) + seq_index * block_width
    shift_table = phase_table(row_index[:, None] * token_index[None, :], fft_length)
    source_rows = (
        jnp.arange(2, dtype=jnp.int32)[:, None] * seq_count
        + jnp.arange(seq_count, dtype=jnp.int32)[None, :]
    )
    zero_block = jnp.zeros_like(slab_rows)
    padded = jnp.stack([jnp.stack([slab_rows, zero_block]), jnp.stack([zero_block, zero_block])])
    pieces = lax.all_to_all(
        padded.reshape(2, 2, all_rows, 1, seq_count, block_width),
        "seq",
        split_axis=4,
        concat_axis=3,
        tiled=True,
    )
    columns = pieces.reshape(2, 2, all_rows, seq_count, block_width)
    tables = phase_table(source_rows[:, :, None] * row_index[None, None, :], freq_rows)
    spectrum = rotate_sum("hxjm,hjk->xkm", (columns[0], columns[1]), tables, -1.0)
    spectrum = rotate(spectrum, shift_table, -1.0)
    stacked = jnp.stack(spectrum).reshape(2, all_rows, freq_rows, 1, block_width)
    row_planes = lax.all_to_all(stacked, "seq", split_axis=2, concat_axis=3, tiled=True)
    planes = row_planes.reshape(2, all_rows, 2, inner_count, block_radix)
    inner_range = jnp.arange(inner_count, dtype=jnp.int32)
    radix_range = jnp.arange(block_radix, dtype=jnp.int32)
    outer_table = phase_table(inner_range[:, None] * inner_range[None, :], inner_count)
    radix_table = phase_table(radix_range[:, None] * radix_range[None, :], block_radix)
    twist_table = phase_table(inner_range[:, None] * radix_range[None, :], tokens)
    spectrum = rotate_sum("xrba,bk->xrka", (planes[0], planes[1]), outer_table, -1.0)
    spectrum = rotate(spectrum, twist_table, -1.0)
    spectrum = rotate_sum("xrka,ac->xrkc", spectrum, radix_table, -1.0)
    sig_real, sig_imag = (spectrum[0][:channels], spectrum[1][:channels])
    fil_real, fil_imag = (spectrum[0][channels:], spectrum[1][channels:])
    spectrum = (
        sig_real * fil_real - sig_imag * fil_imag,
        sig_real * fil_imag + sig_imag * fil_real,
    )
    spectrum = rotate_sum("xrkc,ca->xrka", spectrum, radix_table, 1.0)
    spectrum = rotate(spectrum, twist_table, 1.0)
    spectrum = rotate_sum("xrka,kb->xrba", spectrum, outer_table, 1.0)
    inverse = jnp.stack(spectrum).reshape(2, channels, 2, seq_count, block_width)
    gathered = lax.all_to_all(inverse, "seq", split_axis=3, concat_axis=2, tiled=True)
    gathered = gathered.reshape(2, channels, freq_rows, block_width)
    spectrum = rotate((gathered[0], gathered[1]), shift_table, 1.0)
    tables = phase_table(row_index[:, None, None] * source_rows[None, :, :], freq_rows)
    spectrum = rotate_sum("xkm,khj->xhjm", spectrum, tables, 1.0)
    stacked = jnp.stack(spectrum).reshape(2, channels, 2, seq_count, 1, block_width)
    arrived = lax.all_to_all(stacked, "seq", split_axis=3, concat_axis=4, tiled=True)
    result = arrived[0, :, 0].reshape(channels, tokens)
    return result / fft_length + skip_gain[:, None] * slab_signal


def solution(mesh):
    placed = (P(None, ("seq", "tp")), P(None, ("seq", "tp")), P("tp"))
    return jax.shard_map(
        body, mesh=mesh, in_specs=placed, out_specs=P("tp", "seq"), check_vma=False
    )
```

profile of v0, /device:TPU:1, one launch (start us, length us, event | category | flops | bytes accessed | tf_op | source)
XLA Modules:
  0.0 445.9 jit_solution(14319236365581633981)
XLA Ops:
  0.0 12.5 %all_to_all.89 = f32[4,8,4096]{2,1,0:T(8,128)S(1)} all-to-all(f32[4,8,4096]{2,1,0:T(8,128)} %bitcast.228), channel_id=1, replica_groups=mesh['seq'=64,'tp'=4] {'tp'}, dimensions={0} | all-to-all | bytes 1048576 | tf_op jit(solution)/shard_map/all_to_all | solution.py:41
  12.5 10.4 %all_to_all.90 = f32[4,8,4096]{2,1,0:T(8,128)S(1)} all-to-all(f32[4,8,4096]{2,1,0:T(8,128)} %bitcast.229), channel_id=1, replica_groups=mesh['seq'=64,'tp'=4] {'tp'}, dimensions={0} | all-to-all | bytes 1048576 | tf_op jit(solution)/shard_map/all_to_all | solution.py:42
  22.9 0.1 maximum_bitcast_fusion.2
  23.0 0.1 pad_bitcast_fusion
  23.1 0.3 stack.43
  23.4 1.3 copy.91
  24.6 5.2 %copy.40 = f32[2,2,16,1,64,256]{5,1,2,3,0,4:T(2,128)} copy(f32[2,2,16,1,64,256]{5,4,2,1,0,3:T(8,128)S(1)} %bitcast.221) | data formatting | bytes 8388608 | tf_op jit(solution)/shard_map/reshape | solution.py:61
  29.8 16.7 %all-to-all-start.2 = ((f32[2,2,16,1,64,256]{5,1,2,3,0,4:T(2,128)}), f32[2,2,16,1,64,256]{5,1,2,3,0,4:T(2,128)}, u32[]{:S(2)}, u32[]{:S(2)}) async-start(f32[2,2,16,1,64,256]{5,1,2,3,0,4:T(2,128)} %copy.40), calls=%async_computation.2 | async-start | bytes 8388608 | tf_op jit(solution)/shard_map/all_to_all | solution.py:60
  46.6 0.1 iota_add_fusion.1
  46.6 0.5 fusion.80
  47.2 94.8 %all-to-all-done.2 = f32[2,2,16,1,64,256]{5,1,2,3,0,4:T(2,128)} async-done(((f32[2,2,16,1,64,256]{5,1,2,3,0,4:T(2,128)}), f32[2,2,16,1,64,256]{5,1,2,3,0,4:T(2,128)}, u32[]{:S(2)}, u32[]{:S(2)}) %all-to-all-start.2) | async-done | bytes 4194336 | tf_op jit(solution)/shard_map/all_to_all | solution.py:60
  142.0 3.9 fusion.224
  145.8 3.3 fusion.10
  149.2 3.3 fusion.11
  152.5 3.5 fusion.8
  155.9 4.1 subtract_bitcast_fusion
  160.1 0.5 maximum_bitcast_fusion
  160.5 4.4 copy.43
  164.9 5.9 %all-to-all-start.3 = ((f32[2,16,128,1,256]{4,1,0,3,2:T(8,128)}), f32[2,16,128,1,256]{4,1,0,3,2:T(8,128)}, u32[]{:S(2)}, u32[]{:S(2)}) async-start(f32[2,16,128,1,256]{4,1,0,3,2:T(8,128)} %copy.43), calls=%async_computation.3 | async-start | bytes 8388608 | tf_op jit(solution)/shard_map/all_to_all | solution.py:72
  170.9 0.3 fusion.102
  171.2 0.1 copy.45
  171.2 0.3 broadcast_multiply_fusion.1
  171.5 0.1 copy.46
  171.6 0.3 fusion.101
  171.9 0.1 copy.56
  172.0 94.8 %all-to-all-done.3 = f32[2,16,128,1,256]{4,1,0,3,2:T(8,128)} async-done(((f32[2,16,128,1,256]{4,1,0,3,2:T(8,128)}), f32[2,16,128,1,256]{4,1,0,3,2:T(8,128)}, u32[]{:S(2)}, u32[]{:S(2)}) %all-to-all-start.3) | async-done | bytes 4194336 | tf_op jit(solution)/shard_map/all_to_all | solution.py:72
  266.8 4.6 %copy.122 = f32[2,16,64,2,1,256]{5,2,3,1,4,0:T(8,128)S(1)} copy(f32[2,16,64,2,1,256]{5,1,0,3,2,4:T(8,128)} %bitcast.30) | data formatting | bytes 8388608 | tf_op jit(solution)/shard_map/all_to_all | solution.py:72
  271.4 2.3 fusion.223
  273.7 1.6 squeeze.21
  275.3 3.5 fusion.76
  278.7 3.0 squeeze.20
  281.8 3.8 fusion.78
  285.7 2.3 multiply_add_fusion.2
  288.0 2.3 multiply_subtract_fusion.2
  290.3 2.2 fusion.2
  292.5 2.2 fusion
  294.7 2.4 multiply_subtract_fusion
  297.2 2.3 multiply_add_fusion
  299.4 0.3 multiply_add_fusion.4
  299.8 1.2 fusion.68
  301.0 1.2 fusion.70
  302.2 1.2 convolution_add_fusion.2
  303.5 1.2 convolution_subtract_fusion.2
  304.7 1.3 fusion.34
  306.0 2.3 fusion.35
  308.3 2.5 fusion.21
  310.8 2.5 stack.47
  313.3 3.1 copy.57
  316.4 2.3 fusion.20
  318.8 1.6 stack.48
  320.4 0.8 copy.58
  321.2 1.4 pad_maximum_fusion
  322.6 56.8 %all_to_all.91 = f32[2,8,2,64,256]{4,2,1,0,3:T(2,128)S(1)} all-to-all(f32[2,8,2,64,256]{4,2,1,0,3:T(2,128)S(1)} %pad_maximum_fusion), channel_id=1, replica_groups=mesh['seq'=64,'tp'=4] {'seq'}, dimensions={3} | all-to-all | bytes 4194304 | tf_op jit(solution)/shard_map/all_to_all | solution.py:92
  379.4 0.2 copy.123
  379.6 0.2 fusion.225
  379.8 0.3 fusion.28
  380.1 1.6 fusion.26
  381.7 1.6 fusion.22
  383.3 1.6 fusion.19
  384.9 1.6 fusion.18
  386.4 0.1 maximum_bitcast_fusion.1
  386.6 1.2 copy.64
  387.8 56.9 %all_to_all.92 = f32[2,8,2,64,1,256]{5,1,2,0,4,3:T(8,128)S(1)} all-to-all(f32[2,8,2,64,1,256]{5,1,2,0,4,3:T(8,128)S(1)} %copy.64), channel_id=1, replica_groups=mesh['seq'=64,'tp'=4] {'seq'}, dimensions={3} | all-to-all | bytes 4194304 | tf_op jit(solution)/shard_map/all_to_all | solution.py:98
  444.8 0.9 multiply_add_fusion.7
  (13 shorter events, 0.1 us)
Async XLA Ops:
  29.8 112.1 %all-to-all-start.2 = ((f32[2,2,16,1,64,256]{5,1,2,3,0,4:T(2,128)}), f32[2,2,16,1,64,256]{5,1,2,3,0,4:T(2,128)}, u32[]{:S(2)}, u32[]{:S(2)}) async-start(f32[2,2,16,1,64,256]{5,1,2,3,0,4:T(2,128)} %copy.40), calls=%async_computation.2 | async-start | bytes 8388608 | tf_op jit(solution)/shard_map/all_to_all | solution.py:60
  164.9 101.8 %all-to-all-start.3 = ((f32[2,16,128,1,256]{4,1,0,3,2:T(8,128)}), f32[2,16,128,1,256]{4,1,0,3,2:T(8,128)}, u32[]{:S(2)}, u32[]{:S(2)}) async-start(f32[2,16,128,1,256]{4,1,0,3,2:T(8,128)} %copy.43), calls=%async_computation.3 | async-start | bytes 8388608 | tf_op jit(solution)/shard_map/all_to_all | solution.py:72
  281.8 3.9 copy-start
  281.8 3.9 copy-start.1
  313.3 3.1 copy-start.2
  318.8 2.5 copy-start.3
  387.8 56.9 %copy-start.4 = (f32[8]{0:T(128)S(1)}, f32[8]{0:T(128)}, u32[]{:S(2)}) copy-start(f32[8]{0:T(128)} %param.5) | copy-start | bytes 100
where the time goes:
time: 451 us; the launch traced here: 446 us
  waiting for transfers between devices  190 us (42%)
  blocking collectives  137 us (30%)
  matrix products  54.8 us (12%)
  local copies, waits for them, and re-layouts  36.6 us (8%)
  starting transfers between devices  22.6 us (5%)
  other arithmetic  5.11 us (1%)
    all_to_all x1, waiting for transfers between devices, body(): lax.all_to_all(stacked, 'seq', split_axis=2, concat_axis=3, tiled=True)  94.8 us
    all_to_all x1, waiting for transfers between devices, body(): lax.all_to_all(padded.reshape(2, 2, all_rows, 1, seq_count, block_width),...  94.8 us
    all_to_all x1, blocking collectives, body(): lax.all_to_all(stacked, 'seq', split_axis=3, concat_axis=4, tiled=True)  56.9 us
    all_to_all x1, blocking collectives, body(): lax.all_to_all(inverse, 'seq', split_axis=3, concat_axis=2, tiled=True)  56.8 us
    all_to_all x1, starting transfers between devices, body(): lax.all_to_all(padded.reshape(2, 2, all_rows, 1, seq_count, block_width),...  16.7 us
    dot_general x6, matrix products, rotate_sum(): cos_imag = jnp.einsum(pattern, imag_part, cosine, precision=HIGHEST)  14.2 us
    dot_general x6, matrix products, rotate_sum(): sin_imag = jnp.einsum(pattern, imag_part, sine_table, precision=HIGHEST)  14 us
    dot_general x6, matrix products, rotate_sum(): cos_real = jnp.einsum(pattern, real_part, cosine, precision=HIGHEST)  13.7 us
  transfers between devices with their start and end apart: 2, of which 2 were waited for; matrix products, arithmetic and copies ran while one was open for 0% of the time, Pallas kernels for 0%

commit v1 on v0

--- a/solution.py
+++ b/solution.py
@@ -6,6 +6,22 @@
 
 HIGHEST = lax.Precision.HIGHEST
 block_radix = 128
+
+
+def exchange_in_pairs(shard, axis, split, join):
+    ways, here = (lax.axis_size(axis), lax.axis_index(axis))
+    width = shard.shape[split] // ways
+    dims = list(shard.shape)
+    dims[split] = width
+    height = dims[join]
+    dims[join] = height * ways
+    full = jnp.zeros(dims, shard.dtype)
+    for mask in range(ways):
+        part = lax.dynamic_slice_in_dim(shard, (here ^ mask) * width, width, axis=split)
+        if mask:
+            part = lax.ppermute(part, axis, [(d, d ^ mask) for d in range(ways)])
+        full = lax.dynamic_update_slice_in_dim(full, part, (here ^ mask) * height, axis=join)
+    return full
 
 
 def phase_table(product, modulus):
@@ -38,7 +54,7 @@
     tp_count = lax.axis_size("tp")
     channels = signal.shape[0] // tp_count
     slab_signal, slab_filter = (
-        lax.all_to_all(signal, "tp", split_axis=0, concat_axis=1, tiled=True),
+        exchange_in_pairs(signal, "tp", 0, 1),
         lax.all_to_all(filter_taps, "tp", split_axis=0, concat_axis=1, tiled=True),
     )
     slab_rows = jnp.concatenate([slab_signal, slab_filter], axis=0)

time: 451 us -> 446 us (0.989)
  blocking collectives: 137 us -> 114 us
  waiting for transfers between devices: 190 us -> 198 us
  starting transfers between devices: 22.6 us -> 29.7 us
    all_to_all x2 -> x0, blocking collectives: 22.9 us -> none  [the longest x1 12.5 us: body(): lax.all_to_all(signal, 'tp', split_axis=0, concat_axis=1, tiled=True)]
    ppermute x0 -> x3, starting transfers between devices: none -> 4.62 us  [exchange_in_pairs(): part = lax.ppermute(part, axis, [(d, d ^ mask) for d in range(ways)])]
  transfers between devices with their start and end apart: 2 -> 6, of which waited for: 2 -> 5; matrix products, arithmetic and copies ran while one was open for 0% -> 0% of each run, Pallas kernels for 0% -> 0%
where the time goes in v1:
time: 446 us; the launch traced here: 439 us
  waiting for transfers between devices  198 us (44%)
  blocking collectives  114 us (26%)
  matrix products  54.8 us (12%)
  local copies, waits for them, and re-layouts  37.8 us (8%)
  starting transfers between devices  29.7 us (7%)
  other arithmetic  5.11 us (1%)
    all_to_all x1, waiting for transfers between devices, body(): lax.all_to_all(stacked, 'seq', split_axis=2, concat_axis=3, tiled=True)  94.8 us
    all_to_all x1, waiting for transfers between devices, body(): lax.all_to_all(padded.reshape(2, 2, all_rows, 1, seq_count, block_width),...  94.8 us
    all_to_all x1, blocking collectives, body(): lax.all_to_all(stacked, 'seq', split_axis=3, concat_axis=4, tiled=True)  56.9 us
    all_to_all x1, blocking collectives, body(): lax.all_to_all(inverse, 'seq', split_axis=3, concat_axis=2, tiled=True)  56.8 us
    all_to_all x1, starting transfers between devices, body(): lax.all_to_all(padded.reshape(2, 2, all_rows, 1, seq_count, block_width),...  15.2 us
    dot_general x6, matrix products, rotate_sum(): cos_imag = jnp.einsum(pattern, imag_part, cosine, precision=HIGHEST)  14.2 us
    dot_general x6, matrix products, rotate_sum(): sin_imag = jnp.einsum(pattern, imag_part, sine_table, precision=HIGHEST)  14 us
    dot_general x6, matrix products, rotate_sum(): cos_real = jnp.einsum(pattern, real_part, cosine, precision=HIGHEST)  13.7 us
  transfers between devices with their start and end apart: 6, of which 5 were waited for; matrix products, arithmetic and copies ran while one was open for 0% of the time, Pallas kernels for 0%

profile of v1, /device:TPU:1, one launch (start us, length us, event | category | flops | bytes accessed | tf_op | source)
XLA Modules:
  0.0 439.5 jit_solution(17964783713766148942)
XLA Ops:
  0.0 1.1 constant_dynamic-slice_fusion
  1.2 2.1 collective-permute-start
  3.3 2.5 collective-permute-start.1
  5.8 3.9 all-to-all-start
  9.7 1.7 collective-permute-done.1
  11.5 2.5 collective-permute-done.2
  14.0 3.9 all-to-all-done
  18.0 0.1 pad_bitcast_fusion
  18.1 0.3 stack.43
  18.4 1.3 copy.91
  19.6 5.2 %copy.40 = f32[2,2,16,1,64,256]{5,1,2,3,0,4:T(2,128)} copy(f32[2,2,16,1,64,256]{5,4,2,1,0,3:T(8,128)S(1)} %bitcast.217) | data formatting | bytes 8388608 | tf_op jit(solution)/shard_map/reshape | solution.py:77
  24.9 15.2 %all-to-all-start.1 = ((f32[2,2,16,1,64,256]{5,1,2,3,0,4:T(2,128)}), f32[2,2,16,1,64,256]{5,1,2,3,0,4:T(2,128)}, u32[]{:S(2)}, u32[]{:S(2)}) async-start(f32[2,2,16,1,64,256]{5,1,2,3,0,4:T(2,128)} %copy.40), calls=%async_computation.1 | async-start | bytes 8388608 | tf_op jit(solution)/shard_map/all_to_all | solution.py:76
  40.2 0.5 fusion.80
  40.7 94.8 %all-to-all-done.1 = f32[2,2,16,1,64,256]{5,1,2,3,0,4:T(2,128)} async-done(((f32[2,2,16,1,64,256]{5,1,2,3,0,4:T(2,128)}), f32[2,2,16,1,64,256]{5,1,2,3,0,4:T(2,128)}, u32[]{:S(2)}, u32[]{:S(2)}) %all-to-all-start.1) | async-done | bytes 4194336 | tf_op jit(solution)/shard_map/all_to_all | solution.py:76
  135.5 3.9 fusion.224
  139.4 3.3 fusion.10
  142.7 3.3 fusion.11
  146.0 3.5 fusion.8
  149.5 4.1 subtract_bitcast_fusion
  153.6 0.5 maximum_bitcast_fusion
  154.1 4.4 %copy.43 = f32[2,16,128,1,256]{4,1,0,3,2:T(8,128)} copy(f32[2,16,128,1,256]{4,2,1,0,3:T(8,128)S(1)} %maximum_bitcast_fusion) | data formatting | bytes 8388608 | tf_op jit(solution)/shard_map/reshape | solution.py:87
  158.5 5.9 %all-to-all-start.2 = ((f32[2,16,128,1,256]{4,1,0,3,2:T(8,128)}), f32[2,16,128,1,256]{4,1,0,3,2:T(8,128)}, u32[]{:S(2)}, u32[]{:S(2)}) async-start(f32[2,16,128,1,256]{4,1,0,3,2:T(8,128)} %copy.43), calls=%async_computation.2 | async-start | bytes 8388608 | tf_op jit(solution)/shard_map/all_to_all | solution.py:88
  164.5 0.3 fusion.102
  164.8 0.3 broadcast_multiply_fusion.1
  165.2 0.3 fusion.101
  165.6 94.8 %all-to-all-done.2 = f32[2,16,128,1,256]{4,1,0,3,2:T(8,128)} async-done(((f32[2,16,128,1,256]{4,1,0,3,2:T(8,128)}), f32[2,16,128,1,256]{4,1,0,3,2:T(8,128)}, u32[]{:S(2)}, u32[]{:S(2)}) %all-to-all-start.2) | async-done | bytes 4194336 | tf_op jit(solution)/shard_map/all_to_all | solution.py:88
  260.4 4.6 %copy.122 = f32[2,16,64,2,1,256]{5,2,3,1,4,0:T(8,128)S(1)} copy(f32[2,16,64,2,1,256]{5,1,0,3,2,4:T(8,128)} %bitcast.27) | data formatting | bytes 8388608 | tf_op jit(solution)/shard_map/all_to_all | solution.py:88
  265.0 2.3 fusion.223
  267.2 1.6 squeeze.21
  268.9 3.4 fusion.76
  272.3 3.0 squeeze.20
  275.4 3.8 fusion.78
  279.2 2.3 multiply_add_fusion.2
  281.6 2.3 multiply_subtract_fusion.2
  283.9 2.2 fusion.2
  286.1 2.2 fusion
  288.3 2.4 multiply_subtract_fusion
  290.7 2.3 multiply_add_fusion
  293.0 0.3 multiply_add_fusion.4
  293.4 1.2 fusion.68
  294.6 1.2 fusion.70
  295.8 1.2 convolution_add_fusion.2
  297.0 1.2 convolution_subtract_fusion.2
  298.3 1.3 fusion.34
  299.6 2.3 fusion.35
  301.9 2.5 fusion.21
  304.4 2.5 stack.47
  306.9 3.1 copy.57
  310.0 2.3 fusion.20
  312.3 1.6 stack.48
  314.0 0.8 copy.58
  314.8 1.4 pad_maximum_fusion
  316.2 56.8 %all_to_all.70 = f32[2,8,2,64,256]{4,2,1,0,3:T(2,128)S(1)} all-to-all(f32[2,8,2,64,256]{4,2,1,0,3:T(2,128)S(1)} %pad_maximum_fusion), channel_id=1, replica_groups=mesh['seq'=64,'tp'=4] {'seq'}, dimensions={3} | all-to-all | bytes 4194304 | tf_op jit(solution)/shard_map/all_to_all | solution.py:108
  373.0 0.2 copy.123
  373.2 0.2 fusion.225
  373.4 0.3 fusion.28
  373.7 1.6 fusion.26
  375.3 1.6 fusion.22
  376.8 1.6 fusion.19
  378.4 1.6 fusion.18
  380.0 0.1 maximum_bitcast_fusion.1
  380.2 1.2 copy.64
  381.4 56.9 %all_to_all.71 = f32[2,8,2,64,1,256]{5,1,2,0,4,3:T(8,128)S(1)} all-to-all(f32[2,8,2,64,1,256]{5,1,2,0,4,3:T(8,128)S(1)} %copy.64), channel_id=1, replica_groups=mesh['seq'=64,'tp'=4] {'seq'}, dimensions={3} | all-to-all | bytes 4194304 | tf_op jit(solution)/shard_map/all_to_all | solution.py:114
  438.3 0.9 multiply_add_fusion.7
  (24 shorter events, 0.6 us)
Async XLA Ops:
  1.2 8.5 %collective-permute-start = (f32[8,4096]{1,0:T(8,128)S(1)}, f32[8,4096]{1,0:T(8,128)S(1)}, u32[]{:S(2)}, u32[]{:S(2)}) collective-permute-start(f32[8,4096]{1,0:T(8,128)S(1)} %get-tuple-element.18), channel_id=1, source_target_pairs={{0,1},{1,0},{2,3},{3,2},{4,5},{5,4},{6,7},{7,6},{8,9},{9,8},{10,11... | collective-permute-start | bytes 393224 | tf_op jit(solution)/shard_map/ppermute | solution.py:22
  3.3 8.2 %collective-permute-start.1 = (f32[8,4096]{1,0:T(8,128)S(1)}, f32[8,4096]{1,0:T(8,128)S(1)}, u32[]{:S(2)}, u32[]{:S(2)}) collective-permute-start(f32[8,4096]{1,0:T(8,128)S(1)} %get-tuple-element.20), channel_id=1, source_target_pairs={{0,2},{1,3},{2,0},{3,1},{4,6},{5,7},{6,4},{7,5},{8,10},{9,11},{10,... | collective-permute-start | bytes 393224 | tf_op jit(solution)/shard_map/ppermute | solution.py:22
  5.8 8.2 %collective-permute-start.2 = (f32[8,4096]{1,0:T(8,128)S(1)}, f32[8,4096]{1,0:T(8,128)S(1)}, u32[]{:S(2)}, u32[]{:S(2)}) collective-permute-start(f32[8,4096]{1,0:T(8,128)S(1)} %get-tuple-element.17), channel_id=1, source_target_pairs={{0,3},{1,2},{2,1},{3,0},{4,7},{5,6},{6,5},{7,4},{8,11},{9,10},{10,... | collective-permute-start | bytes 393224 | tf_op jit(solution)/shard_map/ppermute | solution.py:22
  5.8 12.1 %all-to-all-start = ((f32[4,8,4096]{2,1,0:T(8,128)}), f32[4,8,4096]{2,1,0:T(8,128)S(1)}, u32[]{:S(2)}, u32[]{:S(2)}) async-start(f32[4,8,4096]{2,1,0:T(8,128)} %bitcast.222), calls=%async_computation | async-start | bytes 1048576 | tf_op jit(solution)/shard_map/all_to_all | solution.py:58
  24.9 110.7 %all-to-all-start.1 = ((f32[2,2,16,1,64,256]{5,1,2,3,0,4:T(2,128)}), f32[2,2,16,1,64,256]{5,1,2,3,0,4:T(2,128)}, u32[]{:S(2)}, u32[]{:S(2)}) async-start(f32[2,2,16,1,64,256]{5,1,2,3,0,4:T(2,128)} %copy.40), calls=%async_computation.1 | async-start | bytes 8388608 | tf_op jit(solution)/shard_map/all_to_all | solution.py:76
  158.5 101.8 %all-to-all-start.2 = ((f32[2,16,128,1,256]{4,1,0,3,2:T(8,128)}), f32[2,16,128,1,256]{4,1,0,3,2:T(8,128)}, u32[]{:S(2)}, u32[]{:S(2)}) async-start(f32[2,16,128,1,256]{4,1,0,3,2:T(8,128)} %copy.43), calls=%async_computation.2 | async-start | bytes 8388608 | tf_op jit(solution)/shard_map/all_to_all | solution.py:88
  275.3 3.9 copy-start
  275.4 3.9 copy-start.1
  306.9 3.1 copy-start.2
  312.3 2.5 copy-start.3
  381.4 56.9 %copy-start.4 = (f32[8]{0:T(128)S(1)}, f32[8]{0:T(128)}, u32[]{:S(2)}) copy-start(f32[8]{0:T(128)} %param.5) | copy-start | bytes 100
